TPU v7x, 32 devices: a whole 2x2x4 slice. The times are simulated.
32 devices in a mesh: outer: 2 (over x), sec: 8 (over z, core), tp: 2 (over y).
Axes of the slice: x: 2, y: 2, z: 4, core: 2. Of those that a mesh axis runs over, the one named last changes fastest.
Arguments:
- tile_maps: bfloat16 [32, 12, 12, 3072], P(('outer', 'sec'), None, None, 'tp'), may hold values from -6 to 6
- tile_shape: int32 [32, 2], P(('outer', 'sec')), may hold values from 4 to 12
- conv_kernel: float32 [7, 7, 3072], P(None, None, 'tp'), may hold values from -0.875 to 0.875
- norm_gain: float32 [3072], P('tp'), may hold values from 0.25 to 1.75
- norm_bias: float32 [3072], P('tp'), may hold values from -3 to 3
- projector: bfloat16 [3072, 7168], P('tp', 'sec'), may hold values from -0.109375 to 0.109375
- text_rows: bfloat16 [9216, 7168], P(('outer', 'sec'), 'tp'), may hold values from -6 to 6
- row_order: int32 [16, 576], P(('outer', 'sec')), may hold values from 0 to 575, each once within a row
- seq_gain: float32 [7168], P('tp'), may hold values from 0.25 to 1.75
- cotangent: bfloat16 [9216, 7168], P(('outer', 'sec'), 'tp'), may hold values from -0.2772166 to 0.2772166, as said below
Outputs:
- normed: bfloat16 [9216, 7168], P(('outer', 'sec'), 'tp')
- kernel_delta: float32 [7, 7, 3072], P(None, None, 'tp')
- gain_delta: float32 [3072], P('tp')
- bias_delta: float32 [3072], P('tp')
Inputs may be any that keep to these rules, and one draw needn't show every extreme that they name: `row_order`: each row lists where the visual tokens arriving at that device stand, in arrival order, then the text rows. `tile_shape`: valid rows and columns of each tile, the rest of the map is padding. `cotangent`: gradient of the training loss.
All inputs are finite; a program needn't handle non-finite values.
Results may differ from a plain program's by a relative error of at most 0.0043.
Values may be sent and summed in bfloat16 or wider, within the bound.
A program may use at most 128 MiB of HBM per device.

v0:
```python
import jax
import jax.numpy as jnp
from jax import lax
from jax.sharding import PartitionSpec as P


def shape_mask(tile_shape, grid):
    places = lax.broadcasted_iota(jnp.int32, (1, grid), 1)
    rows_ok = places < tile_shape[:, 0:1]
    cols_ok = places < tile_shape[:, 1:2]
    return (rows_ok[:, :, None] & cols_ok[:, None, :]).astype(jnp.float32)


def on_device(
    tile_maps,
    tile_shape,
    conv_kernel,
    norm_gain,
    norm_bias,
    projector,
    text_rows,
    row_order,
    seq_gain,
    cotangent,
):
    grid = tile_maps.shape[1]
    half_ch = tile_maps.shape[3]
    channels = half_ch * lax.axis_size("tp")
    rows_dev = tile_maps.shape[0] * grid * grid
    width = text_rows.shape[1] * lax.axis_size("tp")
    validity = shape_mask(tile_shape, grid)[..., None]
    masked = tile_maps.astype(jnp.float32) * validity
    padded = jnp.pad(masked, ((0, 0), (3, 3), (3, 3), (0, 0)))
    conv_out = jnp.zeros(masked.shape, jnp.float32)
    for row_off in range(7):
        for col_off in range(7):
            conv_out = (
                conv_out
                + padded[:, row_off : row_off + grid, col_off : col_off + grid, :]
                * conv_kernel[row_off, col_off]
            )
    total_one, total_two = lax.psum(
        (jnp.sum(conv_out, axis=-1), jnp.sum(conv_out * conv_out, axis=-1)), "tp"
    )
    center = (total_one / channels)[..., None]
    inverse = lax.rsqrt((total_two / channels)[..., None] - center * center + 1e-06)
    normal = (conv_out - center) * inverse
    features = (
        (validity * (normal * norm_gain + norm_bias))
        .astype(jnp.bfloat16)
        .reshape(rows_dev, half_ch)
    )
    whole_weight = lax.all_gather(projector, "sec", axis=1, tiled=True)
    partial_value = jnp.dot(features, whole_weight, preferred_element_type=jnp.float32)
    visual = lax.psum_scatter(partial_value, "tp", scatter_dimension=1, tiled=True).astype(
        jnp.bfloat16
    )
    arrived = lax.all_to_all(visual, "sec", split_axis=0, concat_axis=0, tiled=True)
    positions = row_order[0, :rows_dev]
    merged = text_rows.at[positions].set(arrived)
    wide = merged.astype(jnp.float32)
    upstream = cotangent.astype(jnp.float32) * seq_gain
    square_sum, along = lax.psum(
        (jnp.sum(wide * wide, axis=-1), jnp.sum(upstream * wide, axis=-1)), "tp"
    )
    inv_rms = lax.rsqrt(square_sum / width + 1e-05)[:, None]
    normed = (wide * inv_rms * seq_gain).astype(jnp.bfloat16)
    grad_seq = inv_rms * upstream - wide * (inv_rms * inv_rms * inv_rms) * along[:, None] / width
    picked = grad_seq[positions].astype(jnp.bfloat16)
    returned = lax.all_to_all(picked, "sec", split_axis=0, concat_axis=0, tiled=True)
    full_grad = lax.all_gather(returned, "tp", axis=1, tiled=True)
    grad_rows = jnp.dot(full_grad, whole_weight.T, preferred_element_type=jnp.float32)
    masked_grad = grad_rows.reshape(masked.shape) * validity
    scaled = masked_grad * norm_gain
    first_sum, second_sum = lax.psum(
        (jnp.sum(scaled, axis=-1), jnp.sum(scaled * normal, axis=-1)), "tp"
    )
    grad_conv = inverse * (
        scaled - (first_sum / channels)[..., None] - normal * (second_sum / channels)[..., None]
    )
    kernel_rows = []
    for row_off in range(7):
        for col_off in range(7):
            window = padded[:, row_off : row_off + grid, col_off : col_off + grid, :]
            kernel_rows.append(jnp.sum(window * grad_conv, axis=(0, 1, 2)))
    gain_grad = jnp.sum(masked_grad * normal, axis=(0, 1, 2))
    bias_grad = jnp.sum(masked_grad, axis=(0, 1, 2))
    local_delta = jnp.stack(kernel_rows + [gain_grad, bias_grad], axis=0)
    pods = lax.axis_size("outer")
    entries = 51 * channels
    pod_sum = lax.psum(local_delta, "sec")
    norm_sq = lax.psum(jnp.sum(pod_sum * pod_sum), "tp")
    factor = jnp.minimum(1.0, 1.0 / jnp.sqrt(norm_sq / entries + 1e-06))
    average = lax.psum(pod_sum * factor, "outer") / pods
    return (normed, average[:49].reshape(7, 7, half_ch), average[49], average[50])


def solution(mesh):
    in_specs = (
        P(("outer", "sec"), None, None, "tp"),
        P(("outer", "sec"), None),
        P(None, None, "tp"),
        P("tp"),
        P("tp"),
        P("tp", "sec"),
        P(("outer", "sec"), "tp"),
        P(("outer", "sec"), None),
        P("tp"),
        P(("outer", "sec"), "tp"),
    )
    out_specs = (P(("outer", "sec"), "tp"), P(None, None, "tp"), P("tp"), P("tp"))
    return jax.shard_map(
        on_device, mesh=mesh, in_specs=in_specs, out_specs=out_specs, check_vma=False
    )
```

profile of v0, /device:TPU:0, one launch (start us, length us, event | category | flops | bytes accessed | tf_op | source)
XLA Modules:
  0.0 696.8 jit_solution(15552070662868830435)
XLA Ops:
  7.2 4.4 copy.23
  11.7 0.6 copy-done.9
  12.3 0.2 slice_reduce_fusion.52
  12.5 0.1 copy-done.2
  12.6 0.2 slice_reduce_fusion.48
  12.8 0.3 slice_reduce_fusion.50
  13.1 0.9 slice_reduce_fusion.49
  14.2 0.2 convert_multiply_fusion.5
  14.4 23.6 %fusion.8 = (f32[2,12,12]{2,1,0:T(8,128)S(1)}, f32[2,12,12]{2,1,0:T(8,128)S(1)}, f32[2,12,12,1536]{3,2,1,0:T(8,128)}) fusion(f32[1536]{0:T(1024)S(1)} %get-tuple-element.110, f32[1536]{0:T(1024)S(1)} %get-tuple-element.111, f32[1536]{0:T(1024)S(1)} %get-tuple-element.64, f32[1536]{0:T(1024)S(1)} %get-tuple-element.65, f32[1536]{0:T(1024)S(1)} %get-tuple-element.66, ...), kind=kLoop, calls=%fused_computation.189 | loop fusion | flops 44236224 | bytes 3842304 | tf_op jit(solution)/shard_map/reduce_sum | solution.py:43
  38.1 9.8 %all-reduce.3 = (f32[2,12,12]{2,1,0:T(8,128)S(1)}, f32[2,12,12]{2,1,0:T(8,128)S(1)}) all-reduce(f32[2,12,12]{2,1,0:T(8,128)S(1)} %get-tuple-element.58, f32[2,12,12]{2,1,0:T(8,128)S(1)} %get-tuple-element.57), channel_id=1, replica_groups=mesh['outer'=2,'sec'=8,'tp'=2] {'tp'}, use_global_device_ids=true, to_apply=%region_3.4 | all-reduce | flops 576 | bytes 4608 | tf_op jit(solution)/shard_map/psum | solution.py:42
  47.9 0.6 copy-done.3
  48.5 3.5 multiply_convert_fusion
  52.0 1.1 reshape.168
  53.1 155.4 %all-gather.3.cloned.1.call-done = bf16[1536,7168]{1,0:T(8,128)(2,1)} async-done(((bf16[1536,896]{1,0:T(8,128)(2,1)}), bf16[1536,7168]{1,0:T(8,128)(2,1)}) %all-gather.3.cloned.1.call-update) | async-done | bytes 22020112 | tf_op jit(solution)/shard_map/all_gather | solution.py:53
  208.5 13.1 %fusion.9 = f32[288,7168]{1,0:T(8,128)} fusion(bf16[288,1536]{1,0:T(8,128)(2,1)} %reshape.168, bf16[1536,7168]{1,0:T(8,128)(2,1)} %all-gather.3.cloned.1.call-done), kind=kOutput, calls=%fused_computation.190 | convolution fusion | flops 6341787648 | bytes 31162368 | tf_op jit(solution)/shard_map/dot_general | solution.py:54
  221.7 96.2 %reduce-scatter.2.cloned.1.call-done = f32[288,3584]{1,0:T(8,128)} async-done(((f32[288,7168]{1,0:T(8,128)}), f32[288,3584]{1,0:T(8,128)}) %reduce-scatter.2.cloned.1.call-update) | async-done | bytes 4128784 | tf_op jit(solution)/shard_map/reduce_scatter | solution.py:55
  317.8 3.7 convert_element_type.43
  321.6 4.0 all_to_all.14
  325.5 4.7 all-to-all-start
  330.3 0.2 all-gather.5.cloned.1.call-start
  330.5 53.1 %all-to-all-done = bf16[8,36,3584]{2,1,0:T(8,128)(2,1)} async-done(((bf16[8,36,3584]{2,1,0:T(8,128)(2,1)}), bf16[8,36,3584]{2,1,0:T(8,128)(2,1)}, u32[]{:S(2)}, u32[]{:S(2)}) %all-to-all-start) | async-done | bytes 2064416 | tf_op jit(solution)/shard_map/all_to_all | solution.py:58
  383.7 4.0 reshape.184
  387.7 9.2 %scatter_fusion = bf16[576,3584]{1,0:T(8,128)(2,1)} fusion(bf16[576,3584]{1,0:T(8,128)(2,1)} %copy.23, s32[288]{0:T(512)S(1)} %fusion.7, bf16[288,3584]{1,0:T(8,128)(2,1)} %reshape.184), kind=kCustom, calls=%fused_computation.1 | custom fusion | bytes 6194304 | tf_op jit(solution)/shard_map/scatter | solution.py:60
  396.9 5.4 fusion.6
  402.3 5.0 all-reduce.2
  407.3 6.7 fusion.5
  414.0 10.0 %gather_fusion = bf16[288,3584]{1,0:T(8,128)(2,1)} fusion(bf16[576,3584]{1,0:T(8,128)(2,1)} %fusion.5, s32[1024]{0:T(1024)S(1)} %pad_clamp_fusion), kind=kCustom, calls=%fused_computation | custom fusion | bytes 4129920 | tf_op jit(solution)/shard_map/gather | solution.py:69
  424.1 4.0 convert_element_type.48
  428.0 57.6 %all_to_all.21 = bf16[8,36,3584]{2,1,0:T(8,128)(2,1)} all-to-all(bf16[8,36,3584]{2,1,0:T(8,128)(2,1)} %convert_element_type.48), channel_id=1, replica_groups=mesh['outer'=2,'sec'=8,'tp'=2] {'sec'}, dimensions={0} | all-to-all | bytes 4128768 | tf_op jit(solution)/shard_map/all_to_all | solution.py:70
  485.7 4.0 all_to_all.18
  489.8 54.0 %all-gather.5.cloned.1.call-done = bf16[288,7168]{1,0:T(8,128)(2,1)} async-done(((bf16[288,3584]{1,0:T(8,128)(2,1)}), bf16[288,7168]{1,0:T(8,128)(2,1)}) %all-gather.5.cloned.1.call-update) | async-done | bytes 4128784 | tf_op jit(solution)/shard_map/all_gather | solution.py:71
  543.7 13.2 %multiply_reduce_fusion.53 = (f32[1536]{0:T(1024)S(1)}, f32[288]{0:T(512)S(1)}, f32[288,1536]{1,0:T(8,128)}) fusion(f32[288]{0:T(512)S(1)} %reshape.171, f32[1536]{0:T(1024)S(1)} %copy-done.8, bf16[288,7168]{1,0:T(8,128)(2,1)} %all-gather.5.cloned.1.call-done, bf16[1536,7168]{1,0:T(8,128)(2,1)} %all-gather.3.cloned.1.call-done), kind=kOutput, calls=%fused_computation.120 | convolution fusion | flops 6343555072 | bytes 27932928 | tf_op jit(solution)/shard_map/dot_general | solution.py:72
  557.0 2.8 reshape.169
  559.8 3.4 multiply_reduce_fusion
  563.2 7.4 %all-reduce.1 = (f32[2,12,12]{2,1,0:T(8,128)S(1)}, f32[2,12,12]{2,1,0:T(8,128)S(1)}) all-reduce(f32[2,12,12]{2,1,0:T(8,128)S(1)} %get-tuple-element.5, f32[2,12,12]{2,1,0:T(8,128)S(1)} %reduce_sum.529), channel_id=1, replica_groups=mesh['outer'=2,'sec'=8,'tp'=2] {'tp'}, use_global_device_ids=true, to_apply=%region_13.14 | all-reduce | flops 576 | bytes 4608 | tf_op jit(solution)/shard_map/psum | solution.py:75
  570.7 9.6 %multiply_reduce_fusion.1 = (f32[1536]{0:T(1024)S(1)}, f32[1536]{0:T(1024)S(1)}, f32[1536]{0:T(1024)S(1)}, f32[1536]{0:T(1024)S(1)}, f32[1536]{0:T(1024)S(1)}, /...) fusion(f32[2,12,12,1536]{3,2,1,0:T(8,128)S(1)} %convert_multipl, ...), kind=kLoop, calls=%fused_computation.63 | loop fusion | flops 19436544 | bytes 7200384 | tf_op jit(solution)/shard_map/reduce_sum | solution.py:85
  580.3 6.3 multiply_reduce_fusion.19
  586.6 5.4 multiply_reduce_fusion.38
  592.8 4.8 stack.207
  597.7 54.4 %all-reduce.7.cloned.1.call-done = f32[51,1536]{1,0:T(8,128)} async-done(((f32[51,1536]{1,0:T(8,128)}), f32[51,1536]{1,0:T(8,128)}) %all-reduce.7.cloned.1.call-update) | async-done | bytes 313360 | tf_op jit(solution)/shard_map/psum | solution.py:91
  652.0 1.7 multiply_reduce_fusion.54
  653.7 5.5 psum.70
  660.0 1.7 broadcast_multiply_fusion.1
  661.7 5.5 fusion.2
  667.2 20.6 %all-reduce.9.cloned.1.call-done = f32[51,1536]{1,0:T(8,128)} async-done(((f32[51,1536]{1,0:T(8,128)}), f32[51,1536]{1,0:T(8,128)}) %all-reduce.9.cloned.1.call-update) | async-done | bytes 313360 | tf_op jit(solution)/shard_map/psum | solution.py:94
  687.9 1.0 broadcast_multiply_fusion
  688.9 0.6 slice_reduce_fusion
  689.5 0.8 reshape.170
  (89 shorter events, 1.0 us)
Async XLA Ops:
  7.2 201.4 %all-gather.3.cloned.1.call-start = ((), (), s32[]{:S(2)}) async-start(), calls=%async_computation.3 | async-start | bytes 24772608 | tf_op jit(solution)/shard_map/all_gather | solution.py:53
  11.6 0.7 copy-start.9
  11.6 1.0 copy-start.2
  11.6 2.6 copy-start
  11.7 306.2 %reduce-scatter.2.cloned.1.call-start = ((), (), s32[]{:S(2)}) async-start(), calls=%async_computation.4 | async-start | bytes 12386304 | tf_op jit(solution)/shard_map/reduce_scatter | solution.py:55
  47.9 0.6 copy-start.3
  47.9 0.6 copy-start.5
  325.5 5.0 copy-start.10
  325.5 58.1 %all-to-all-start = ((bf16[8,36,3584]{2,1,0:T(8,128)(2,1)}), bf16[8,36,3584]{2,1,0:T(8,128)(2,1)}, u32[]{:S(2)}, u32[]{:S(2)}) async-start(bf16[8,36,3584]{2,1,0:T(8,128)(2,1)} %all_to_all.14), calls=%async_computation.1 | async-start | bytes 4587520 | tf_op jit(solution)/shard_map/all_to_all | solution.py:58
  330.3 213.5 %all-gather.5.cloned.1.call-start = ((), (), s32[]{:S(2)}) async-start(), calls=%async_computation.5 | async-start | bytes 6193152 | tf_op jit(solution)/shard_map/all_gather | solution.py:71
  387.7 9.2 %copy-start.7 = (f32[3584]{0:T(1024)S(1)}, f32[3584]{0:T(1024)}, u32[]{:S(2)}) copy-start(f32[3584]{0:T(1024)} %param.18) | copy-start | bytes 43012
  485.6 58.1 %copy-start.8 = (f32[1536]{0:T(1024)S(1)}, f32[1536]{0:T(1024)}, u32[]{:S(2)}) copy-start(f32[1536]{0:T(1024)} %param.13) | copy-start | bytes 18436
  489.6 162.4 %all-reduce.7.cloned.1.call-start = ((), (), s32[]{:S(2)}) async-start(), calls=%async_computation.6 | async-start | bytes 688128 | tf_op jit(solution)/shard_map/psum | solution.py:91
  557.0 2.8 copy-start.4
  557.0 2.8 copy-start.6
  580.3 6.4 copy-start.1
  597.6 90.2 %all-reduce.9.cloned.1.call-start = ((), (), s32[]{:S(2)}) async-start(), calls=%async_computation.7 | async-start | bytes 688128 | tf_op jit(solution)/shard_map/psum | solution.py:94
Sparse Core Ops, SparseCore 0:
  11.8 196.7 all-gather.2
  221.8 96.0 reduce-scatter.1
  489.8 53.9 all-gather.4
  597.7 54.2 all-reduce.6
  661.8 25.9 all-reduce.8
where the time goes:
time: 698 us; the launch traced here: 697 us
  waiting for transfers between devices  434 us (62%)
  blocking collectives  85.4 us (12%)
  other arithmetic  78 us (11%)
  local copies, waits for them, and re-layouts  53.2 us (8%)
  matrix products  26.4 us (4%)
  between operations  15 us (2%)
    all_gather x1, waiting for transfers between devices, on_device(): whole_weight = lax.all_gather(projector, 'sec', axis=1, tiled=True)  155 us
    reduce_scatter x1, waiting for transfers between devices, on_device(): lax.psum_scatter(partial_value, 'tp', scatter_dimension=1, tiled=True)  96.2 us
    all_to_all x1, blocking collectives, on_device(): lax.all_to_all(picked, 'sec', split_axis=0, concat_axis=0, tiled=True)  57.6 us
    psum x1, waiting for transfers between devices, on_device(): pod_sum = lax.psum(local_delta, 'sec')  54.4 us
    all_gather x1, waiting for transfers between devices, on_device(): full_grad = lax.all_gather(returned, 'tp', axis=1, tiled=True)  54 us
    all_to_all x1, waiting for transfers between devices, on_device(): lax.all_to_all(visual, 'sec', split_axis=0, concat_axis=0, tiled=True)  53.1 us
    reduce_sum x1, other arithmetic, on_device(): jnp.sum(conv_out, axis=-1)  23.6 us
    reduce_sum x3, other arithmetic, on_device(): kernel_rows.append(jnp.sum(window * grad_conv, axis=(0, 1, 2)))  21.3 us
  transfers between devices with their start and end apart: 6, of which 6 were waited for; matrix products, arithmetic and copies ran while one was open for 5% of the time, Pallas kernels for 0%

commit v1 on v0

--- a/solution.py
+++ b/solution.py
@@ -2,6 +2,7 @@
 import jax.numpy as jnp
 from jax import lax
 from jax.sharding import PartitionSpec as P
+from jax.lax import axis_index, ppermute, psum
 
 
 def shape_mask(tile_shape, grid):
@@ -50,7 +51,23 @@
         .astype(jnp.bfloat16)
         .reshape(rows_dev, half_ch)
     )
-    whole_weight = lax.all_gather(projector, "sec", axis=1, tiled=True)
+
+    def apply_pools(view, mesh_dim):
+        many = psum(1, axis_name=mesh_dim)
+        line_up = [(k0, (k0 + 1) % many) for k0 in range(many)]
+        gallery = [(k0, (k0 - 1) % many) for k0 in range(many)]
+        reply, near = ([view], [view])
+        for _ in range(many // 2):
+            u1 = ppermute(reply[-1], axis_name=mesh_dim, perm=line_up)
+            reply.append(u1)
+        for _ in [*range((many - 1) // 2)]:
+            g_now = ppermute(near[-1], perm=gallery, axis_name=mesh_dim)
+            near.append(g_now)
+        piece_now = jnp.concatenate([*reply[::-1], *near[1:]], axis=1)
+        seen_now = axis_index(mesh_dim)
+        return jnp.roll(piece_now, (seen_now - many // 2) * view.shape[1], axis=1)
+
+    whole_weight = apply_pools(projector, "sec")
     partial_value = jnp.dot(features, whole_weight, preferred_element_type=jnp.float32)
     visual = lax.psum_scatter(partial_value, "tp", scatter_dimension=1, tiled=True).astype(
         jnp.bfloat16

time: 698 us -> 771 us (1.10)
  local copies, waits for them, and re-layouts: 53.2 us -> 111 us
  starting transfers between devices: 5.12 us -> 14.9 us
    all_gather x1 -> x0, waiting for transfers between devices: 155 us -> none  [on_device(): whole_weight = lax.all_gather(projector, 'sec', axis=1, tiled=True)]
    ppermute x0 -> x7, waiting for transfers between devices: none -> 150 us  [the longest x4 148 us: apply_pools(): u1 = ppermute(reply[-1], axis_name=mesh_dim, perm=line_up)]
    unnamed x23 -> x42, local copies, waits for them, and re-layouts: 5.79 us -> 57 us
    ppermute x0 -> x7, starting transfers between devices: none -> 9.46 us  [the longest x3 9 us: apply_pools(): g_now = ppermute(near[-1], perm=gallery, axis_name=mesh_dim)]
  transfers between devices with their start and end apart: 6 -> 12, of which waited for: 6 -> 9; matrix products, arithmetic and copies ran while one was open for 5% -> 8% of each run, Pallas kernels for 0% -> 0%
where the time goes in v1:
time: 771 us; the launch traced here: 765 us
  waiting for transfers between devices  431 us (56%)
  local copies, waits for them, and re-layouts  111 us (14%)
  blocking collectives  86.6 us (11%)
  other arithmetic  76.3 us (10%)
  matrix products  29.5 us (4%)
  between operations  15.3 us (2%)
  starting transfers between devices  14.9 us (2%)
    ppermute x4, waiting for transfers between devices, apply_pools(): u1 = ppermute(reply[-1], axis_name=mesh_dim, perm=line_up)  148 us
    reduce_scatter x1, waiting for transfers between devices, on_device(): lax.psum_scatter(partial_value, 'tp', scatter_dimension=1, tiled=True)  98.7 us
    all_to_all x1, blocking collectives, on_device(): lax.all_to_all(picked, 'sec', split_axis=0, concat_axis=0, tiled=True)  57.6 us
    unnamed x42, local copies, waits for them, and re-layouts  57 us
    psum x1, waiting for transfers between devices, on_device(): pod_sum = lax.psum(local_delta, 'sec')  54.4 us
    all_gather x1, waiting for transfers between devices, on_device(): full_grad = lax.all_gather(returned, 'tp', axis=1, tiled=True)  54 us
    all_to_all x1, waiting for transfers between devices, on_device(): lax.all_to_all(visual, 'sec', split_axis=0, concat_axis=0, tiled=True)  52.8 us
    reduce_sum x1, other arithmetic, on_device(): jnp.sum(conv_out, axis=-1)  22 us
  transfers between devices with their start and end apart: 12, of which 9 were waited for; matrix products, arithmetic and copies ran while one was open for 8% of the time, Pallas kernels for 0%

profile of v1, /device:TPU:0, one launch (start us, length us, event | category | flops | bytes accessed | tf_op | source)
XLA Modules:
  0.0 764.8 jit_solution(1421490677734513257)
XLA Ops:
  7.2 4.5 copy.38
  12.2 35.0 %collective-permute-done = bf16[1536,896]{1,0:T(8,128)(2,1)S(1)} collective-permute-done((bf16[1536,896]{1,0:T(8,128)(2,1)}, bf16[1536,896]{1,0:T(8,128)(2,1)S(1)}, u32[]{:S(2)}, u32[]{:S(2)}) %collective-permute-start) | collective-permute-done | bytes 2752544 | tf_op jit(solution)/shard_map/ppermute | solution.py:61
  48.7 3.5 collective-permute-start.4
  52.2 59.4 %collective-permute-done.1 = bf16[1536,896]{1,0:T(8,128)(2,1)} collective-permute-done((bf16[1536,896]{1,0:T(8,128)(2,1)S(1)}, bf16[1536,896]{1,0:T(8,128)(2,1)}, u32[]{:S(2)}, u32[]{:S(2)}) %collective-permute-start.1) | collective-permute-done | bytes 2752544 | tf_op jit(solution)/shard_map/ppermute | solution.py:61
  114.1 3.6 collective-permute-start.5
  120.7 53.2 %collective-permute-done.2 = bf16[1536,896]{1,0:T(8,128)(2,1)} collective-permute-done((bf16[1536,896]{1,0:T(8,128)(2,1)}, bf16[1536,896]{1,0:T(8,128)(2,1)}, u32[]{:S(2)}, u32[]{:S(2)}) %collective-permute-start.2) | collective-permute-done | bytes 2752544 | tf_op jit(solution)/shard_map/ppermute | solution.py:61
  173.9 22.0 %fusion.14 = (f32[2,12,12]{2,1,0:T(8,128)S(1)}, f32[2,12,12]{2,1,0:T(8,128)S(1)}, f32[2,12,12,1536]{3,2,1,0:T(8,128)}) fusion(f32[1536]{0:T(1024)S(1)} %get-tuple-element.110, f32[1536]{0:T(1024)S(1)} %get-tuple-element.111, f32[1536]{0:T(1024)S(1)} %get-tuple-element.64, f32[1536]{0:T(1024)S(1)} %get-tuple-element.65, f32[1536]{0:T(1024)S(1)} %get-tuple-element.66, ...), kind=kLoop, calls=%fused_computation.211 | loop fusion | flops 44236224 | bytes 3842304 | tf_op jit(solution)/shard_map/reduce_sum | solution.py:44
  195.9 10.9 %all-reduce.3 = (f32[2,12,12]{2,1,0:T(8,128)S(1)}, f32[2,12,12]{2,1,0:T(8,128)S(1)}) all-reduce(f32[2,12,12]{2,1,0:T(8,128)S(1)} %get-tuple-element.58, f32[2,12,12]{2,1,0:T(8,128)S(1)} %get-tuple-element.57), channel_id=1, replica_groups=mesh['outer'=2,'sec'=8,'tp'=2] {'tp'}, use_global_device_ids=true, to_apply=%region_3.4 | all-reduce | flops 576 | bytes 4608 | tf_op jit(solution)/shard_map/psum | solution.py:43
  213.3 3.7 constant_dynamic-update-slice_fusion.15
  217.0 3.6 constant_dynamic-update-slice_fusion.14
  220.7 3.8 constant_dynamic-update-slice_fusion.13
  226.3 3.6 constant_dynamic-update-slice_fusion.11
  229.9 3.6 constant_dynamic-update-slice_fusion.10
  233.5 3.6 constant_dynamic-update-slice_fusion.9
  239.6 3.6 constant_dynamic-update-slice_fusion.8
  243.2 3.6 constant_dynamic-update-slice_fusion.7
  246.8 3.7 constant_dynamic-update-slice_fusion.6
  250.4 3.7 constant_dynamic-update-slice_fusion.5
  256.0 3.6 constant_dynamic-update-slice_fusion.3
  259.6 3.6 constant_dynamic-update-slice_fusion.2
  263.2 3.6 constant_dynamic-update-slice_fusion.1
  266.8 3.8 constant_dynamic-update-slice_fusion
  270.5 14.1 %fusion.2 = f32[288,7168]{1,0:T(8,128)} fusion(bf16[288,1536]{1,0:T(8,128)(2,1)S(1)} %copy-done.4, bf16[1536,14336]{1,0:T(8,128)(2,1)} %constant_dynamic-update-slice_fusion, s32[]{:T(128)S(6)} %select_n.26), kind=kOutput, calls=%fused_computation.52 | convolution fusion | flops 6341787648 | bytes 31162372 | tf_op jit(solution)/shard_map/dot_general | solution.py:71
  284.6 98.7 %reduce-scatter.2.cloned.1.call-done = f32[288,3584]{1,0:T(8,128)} async-done(((f32[288,7168]{1,0:T(8,128)}), f32[288,3584]{1,0:T(8,128)}) %reduce-scatter.2.cloned.1.call-update) | async-done | bytes 4128784 | tf_op jit(solution)/shard_map/reduce_scatter | solution.py:72
  383.3 3.7 convert_element_type.43
  387.0 4.0 all_to_all.14
  391.0 4.7 all-to-all-start
  396.3 52.8 %all-to-all-done = bf16[8,36,3584]{2,1,0:T(8,128)(2,1)} async-done(((bf16[8,36,3584]{2,1,0:T(8,128)(2,1)}), bf16[8,36,3584]{2,1,0:T(8,128)(2,1)}, u32[]{:S(2)}, u32[]{:S(2)}) %all-to-all-start) | async-done | bytes 2064416 | tf_op jit(solution)/shard_map/all_to_all | solution.py:75
  449.1 4.0 reshape.184
  453.1 9.2 %scatter_fusion = bf16[576,3584]{1,0:T(8,128)(2,1)} fusion(bf16[576,3584]{1,0:T(8,128)(2,1)} %copy.38, s32[288]{0:T(512)S(1)} %fusion.11, bf16[288,3584]{1,0:T(8,128)(2,1)} %reshape.184), kind=kCustom, calls=%fused_computation.1 | custom fusion | bytes 6194304 | tf_op jit(solution)/shard_map/scatter | solution.py:77
  462.3 5.4 fusion.10
  467.7 5.2 all-reduce.2
  472.8 6.7 fusion.9
  479.5 10.0 %gather_fusion = bf16[288,3584]{1,0:T(8,128)(2,1)} fusion(bf16[576,3584]{1,0:T(8,128)(2,1)} %fusion.9, s32[1024]{0:T(1024)S(1)} %pad_clamp_fusion), kind=kCustom, calls=%fused_computation | custom fusion | bytes 4129920 | tf_op jit(solution)/shard_map/gather | solution.py:86
  489.6 3.9 convert_element_type.48
  493.5 57.6 %all_to_all.21 = bf16[8,36,3584]{2,1,0:T(8,128)(2,1)} all-to-all(bf16[8,36,3584]{2,1,0:T(8,128)(2,1)} %convert_element_type.48), channel_id=1, replica_groups=mesh['outer'=2,'sec'=8,'tp'=2] {'sec'}, dimensions={0} | all-to-all | bytes 4128768 | tf_op jit(solution)/shard_map/all_to_all | solution.py:87
  551.2 4.0 all_to_all.18
  555.3 54.0 %all-gather.2.cloned.1.call-done = bf16[288,7168]{1,0:T(8,128)(2,1)} async-done(((bf16[288,3584]{1,0:T(8,128)(2,1)}), bf16[288,7168]{1,0:T(8,128)(2,1)}) %all-gather.2.cloned.1.call-update) | async-done | bytes 4128784 | tf_op jit(solution)/shard_map/all_gather | solution.py:88
  609.2 15.5 %multiply_reduce_fusion.53 = (f32[1536]{0:T(1024)S(1)}, f32[288]{0:T(512)S(1)}, f32[288,1536]{1,0:T(8,128)}) fusion(f32[288]{0:T(512)S(1)} %reshape.171, f32[1536]{0:T(1024)S(1)} %copy-done.10, bf16[288,7168]{1,0:T(8,128)(2,1)} %all-gather.2.cloned.1.call-done, bf16[1536,14336]{1,0:T(8,128)(2,1)} %constant_dynamic-update-slice_fusion, s32[]{:T(128)S(6)} %select_n.26), kind=kOutput, calls=%fused_computation.124 | convolution fusion | flops 6343555072 | bytes 27932932 | tf_op jit(solution)/shard_map/dot_general | solution.py:89
  630.9 7.4 all-reduce.1
  638.4 9.6 %multiply_reduce_fusion.1 = (f32[1536]{0:T(1024)S(1)}, f32[1536]{0:T(1024)S(1)}, f32[1536]{0:T(1024)S(1)}, f32[1536]{0:T(1024)S(1)}, f32[1536]{0:T(1024)S(1)}, /...) fusion(f32[2,12,12,1536]{3,2,1,0:T(8,128)S(1)} %convert_multipl, ...), kind=kLoop, calls=%fused_computation.67 | loop fusion | flops 19436544 | bytes 7200384 | tf_op jit(solution)/shard_map/reduce_sum | solution.py:102
  647.9 6.3 multiply_reduce_fusion.19
  654.3 5.4 multiply_reduce_fusion.38
  660.5 4.8 stack.207
  665.3 54.4 %all-reduce.7.cloned.1.call-done = f32[51,1536]{1,0:T(8,128)} async-done(((f32[51,1536]{1,0:T(8,128)}), f32[51,1536]{1,0:T(8,128)}) %all-reduce.7.cloned.1.call-update) | async-done | bytes 313360 | tf_op jit(solution)/shard_map/psum | solution.py:108
  721.5 5.5 psum.70
  729.5 5.5 fusion.6
  735.0 20.6 %all-reduce.9.cloned.1.call-done = f32[51,1536]{1,0:T(8,128)} async-done(((f32[51,1536]{1,0:T(8,128)}), f32[51,1536]{1,0:T(8,128)}) %all-reduce.9.cloned.1.call-update) | async-done | bytes 313360 | tf_op jit(solution)/shard_map/psum | solution.py:111
  (120 shorter events, 33.4 us)
Async XLA Ops:
  7.2 106.6 %copy-start.2 = (bf16[2,12,12,1536]{3,0,2,1:T(2,128)(2,1)S(1)}, bf16[2,12,12,1536]{3,0,2,1:T(2,128)(2,1)}, u32[]{:S(2)}) copy-start(bf16[2,12,12,1536]{3,0,2,1:T(2,128)(2,1)} %param.10) | copy-start | bytes 2654212
  7.2 104.5 %copy-start.11 = (s32[2,2]{1,0:T(2,128)S(1)}, s32[2,2]{1,0:T(2,128)}, u32[]{:S(2)}) copy-start(s32[2,2]{1,0:T(2,128)} %param.11) | copy-start | bytes 52
  7.2 376.1 %reduce-scatter.2.cloned.1.call-start = ((), (), s32[]{:S(2)}) async-start(), calls=%async_computation.3 | async-start | bytes 12386304 | tf_op jit(solution)/shard_map/reduce_scatter | solution.py:72
  11.7 35.4 %collective-permute-start = (bf16[1536,896]{1,0:T(8,128)(2,1)}, bf16[1536,896]{1,0:T(8,128)(2,1)S(1)}, u32[]{:S(2)}, u32[]{:S(2)}) collective-permute-start(bf16[1536,896]{1,0:T(8,128)(2,1)} %param.15), channel_id=1, source_target_pairs={{0,2},{2,4},{4,6},{6,8},{8,10},{10,12},{12,14},{14,0},{1,3},{3,5},... | collective-permute-start | bytes 8257544 | tf_op jit(solution)/shard_map/ppermute | solution.py:61
  47.2 1.5 copy-start
  48.7 63.0 %collective-permute-start.1 = (bf16[1536,896]{1,0:T(8,128)(2,1)S(1)}, bf16[1536,896]{1,0:T(8,128)(2,1)}, u32[]{:S(2)}, u32[]{:S(2)}) collective-permute-start(bf16[1536,896]{1,0:T(8,128)(2,1)S(1)} %collective-permute-done), channel_id=1, source_target_pairs={{0,2},{2,4},{4,6},{6,8},{8,10},{10,12},{12,14},{14,0},{1,3},{3,5},... | collective-permute-start | bytes 8257544 | tf_op jit(solution)/shard_map/ppermute | solution.py:61
  48.7 65.4 %collective-permute-start.4 = (bf16[1536,896]{1,0:T(8,128)(2,1)}, bf16[1536,896]{1,0:T(8,128)(2,1)}, u32[]{:S(2)}, u32[]{:S(2)}) collective-permute-start(bf16[1536,896]{1,0:T(8,128)(2,1)} %param.15), channel_id=1, source_target_pairs={{0,14},{2,0},{4,2},{6,4},{8,6},{10,8},{12,10},{14,12},{1,15},{3,1}... | collective-permute-start | bytes 8257544 | tf_op jit(solution)/shard_map/ppermute | solution.py:64
  111.6 62.3 %collective-permute-start.2 = (bf16[1536,896]{1,0:T(8,128)(2,1)}, bf16[1536,896]{1,0:T(8,128)(2,1)}, u32[]{:S(2)}, u32[]{:S(2)}) collective-permute-start(bf16[1536,896]{1,0:T(8,128)(2,1)} %collective-permute-done.1), channel_id=1, source_target_pairs={{0,2},{2,4},{4,6},{6,8},{8,10},{10,12},{12,14},{14,0},{1,3},{3,5},... | collective-permute-start | bytes 8257544 | tf_op jit(solution)/shard_map/ppermute | solution.py:61
  114.1 92.8 %collective-permute-start.5 = (bf16[1536,896]{1,0:T(8,128)(2,1)}, bf16[1536,896]{1,0:T(8,128)(2,1)}, u32[]{:S(2)}, u32[]{:S(2)}) collective-permute-start(bf16[1536,896]{1,0:T(8,128)(2,1)} %collective-permute-done.4), channel_id=1, source_target_pairs={{0,14},{2,0},{4,2},{6,4},{8,6},{10,8},{12,10},{14,12},{1,15},{3,1}... | collective-permute-start | bytes 8257544 | tf_op jit(solution)/shard_map/ppermute | solution.py:64
  173.9 39.4 %collective-permute-start.3 = (bf16[1536,896]{1,0:T(8,128)(2,1)}, bf16[1536,896]{1,0:T(8,128)(2,1)}, u32[]{:S(2)}, u32[]{:S(2)}) collective-permute-start(bf16[1536,896]{1,0:T(8,128)(2,1)} %collective-permute-done.2), channel_id=1, source_target_pairs={{0,2},{2,4},{4,6},{6,8},{8,10},{10,12},{12,14},{14,0},{1,3},{3,5},... | collective-permute-start | bytes 8257544 | tf_op jit(solution)/shard_map/ppermute | solution.py:61
  206.8 1.9 copy-start.5
  206.8 1.9 copy-start.7
  206.8 32.8 %collective-permute-start.6 = (bf16[1536,896]{1,0:T(8,128)(2,1)}, bf16[1536,896]{1,0:T(8,128)(2,1)}, u32[]{:S(2)}, u32[]{:S(2)}) collective-permute-start(bf16[1536,896]{1,0:T(8,128)(2,1)} %collective-permute-done.5), channel_id=1, source_target_pairs={{0,14},{2,0},{4,2},{6,4},{8,6},{10,8},{12,10},{14,12},{1,15},{3,1}... | collective-permute-start | bytes 8257544 | tf_op jit(solution)/shard_map/ppermute | solution.py:64
  220.7 3.8 copy-start.1
  266.8 3.8 copy-start.4
  391.0 5.3 copy-start.12
  391.0 58.1 %all-to-all-start = ((bf16[8,36,3584]{2,1,0:T(8,128)(2,1)}), bf16[8,36,3584]{2,1,0:T(8,128)(2,1)}, u32[]{:S(2)}, u32[]{:S(2)}) async-start(bf16[8,36,3584]{2,1,0:T(8,128)(2,1)} %all_to_all.14), calls=%async_computation.1 | async-start | bytes 4587520 | tf_op jit(solution)/shard_map/all_to_all | solution.py:75
  395.7 213.5 %all-gather.2.cloned.1.call-start = ((), (), s32[]{:S(2)}) async-start(), calls=%async_computation.4 | async-start | bytes 6193152 | tf_op jit(solution)/shard_map/all_gather | solution.py:88
  453.1 9.2 %copy-start.9 = (f32[3584]{0:T(1024)S(1)}, f32[3584]{0:T(1024)}, u32[]{:S(2)}) copy-start(f32[3584]{0:T(1024)} %param.18) | copy-start | bytes 43012
  551.2 58.1 %copy-start.10 = (f32[1536]{0:T(1024)S(1)}, f32[1536]{0:T(1024)}, u32[]{:S(2)}) copy-start(f32[1536]{0:T(1024)} %param.13) | copy-start | bytes 18436
  555.1 164.7 %all-reduce.7.cloned.1.call-start = ((), (), s32[]{:S(2)}) async-start(), calls=%async_computation.5 | async-start | bytes 688128 | tf_op jit(solution)/shard_map/psum | solution.py:108
  624.7 2.8 copy-start.6
  624.7 2.8 copy-start.8
  647.9 6.4 copy-start.3
  665.3 90.3 %all-reduce.9.cloned.1.call-start = ((), (), s32[]{:S(2)}) async-start(), calls=%async_computation.6 | async-start | bytes 688128 | tf_op jit(solution)/shard_map/psum | solution.py:111
Sparse Core Ops, SparseCore 0:
  284.7 98.5 reduce-scatter.1
  555.3 53.9 all-gather.1
  665.4 54.3 all-reduce.6
  729.6 25.9 all-reduce.8
